TPU v7x, 32 devices: a whole 2x2x4 slice. The times are simulated.
32 devices in a mesh: fsdp: 8 (over z, y), seq: 4 (over x, core).
Axes of the slice: x: 2, y: 2, z: 4, core: 2. Of those that a mesh axis runs over, the one named last changes fastest.
Arguments:
- latents: bfloat16 [16, 512, 1152], P('fsdp', 'seq'), may hold values from -6 to 6
- condition: bfloat16 [16, 1152], P('fsdp'), may hold values from -6 to 6
- mod_weight: bfloat16 [1152, 6912], P('fsdp'), may hold values from -0.1875 to 0.1875
- mod_bias: bfloat16 [6912], P('fsdp'), may hold values from -4 to 4
- qkv_weight: bfloat16 [1152, 3456], P('fsdp'), may hold values from -0.1875 to 0.1875
- qv_bias: bfloat16 [2304], P('fsdp'), may hold values from -4 to 4
- out_weight: bfloat16 [1152, 1152], P('fsdp'), may hold values from -1.5 to 1.5
- out_bias: bfloat16 [1152], P('fsdp'), may hold values from -4 to 4
- up_weight: bfloat16 [1152, 4608], P('fsdp'), may hold values from -0.1875 to 0.1875
- up_bias: bfloat16 [4608], P('fsdp'), may hold values from -4 to 4
- down_weight: bfloat16 [4608, 1152], P('fsdp'), may hold values from -0.09375 to 0.09375
- down_bias: bfloat16 [1152], P('fsdp'), may hold values from -4 to 4
- cotangent: bfloat16 [16, 512, 1152], P('fsdp', 'seq'), may hold values from -6 to 6
Outputs:
- mixed: bfloat16 [16, 512, 1152], P('fsdp', 'seq')
- grad_latents: float32 [16, 512, 1152], P('fsdp', 'seq')
- grad_condition: float32 [16, 1152], P('fsdp')
- grad_mod_weight: float32 [1152, 6912], P('fsdp')
- grad_mod_bias: float32 [6912], P('fsdp')
- grad_qkv_weight: float32 [1152, 3456], P('fsdp')
- grad_qv_bias: float32 [2304], P('fsdp')
- grad_out_weight: float32 [1152, 1152], P('fsdp')
- grad_out_bias: float32 [1152], P('fsdp')
- grad_up_weight: float32 [1152, 4608], P('fsdp')
- grad_up_bias: float32 [4608], P('fsdp')
- grad_down_weight: float32 [4608, 1152], P('fsdp')
- grad_down_bias: float32 [1152], P('fsdp')
All inputs are finite; a program needn't handle non-finite values.
Results may differ from a plain program's by a relative error of at most 0.015.
The roundings to bfloat16 on the way count: a program that leaves them out, or rounds other values in their place, can miss the bound.
Values may be sent and summed in bfloat16 or wider, within the bound.
No kernel may reach another device: no remote copies, remote signals or barrier semaphores. Data moves between devices by JAX's collectives and lax.ppermute only.
A program may use at most 256 MiB of HBM per device.

v0:
```python
import jax
import jax.numpy as jnp
from jax import lax
from jax.sharding import PartitionSpec as P

H = 16
HD = 72


def normalize(values):
    centre = values - jnp.mean(values, axis=-1, keepdims=True)
    spread = jnp.mean(centre * centre, axis=-1, keepdims=True)
    return centre * lax.rsqrt(spread + 1e-06)


def matmul(left_side, right_side):
    return jnp.dot(left_side, right_side, preferred_element_type=jnp.float32)


def left_inner(left_side, right_side):
    return lax.dot_general(
        left_side, right_side, (((0,), (0,)), ((), ())), preferred_element_type=jnp.float32
    )


def right_inner(left_side, right_side):
    return lax.dot_general(
        left_side, right_side, (((1,), (1,)), ((), ())), preferred_element_type=jnp.float32
    )


def attend(queries, keys_all, values_all, block_rows, factor):
    length, head_count, head_width = queries.shape
    blocks = queries.reshape(length // block_rows, block_rows, head_count, head_width)

    def one_block(query_block):
        scores = (
            jnp.einsum("qhd,khd->hqk", query_block, keys_all, preferred_element_type=jnp.float32)
            * factor
        )
        highest = jnp.max(scores, axis=-1, keepdims=True)
        raised = jnp.exp(scores - highest)
        totals = jnp.sum(raised, axis=-1, keepdims=True)
        probabilities = (raised / totals).astype(jnp.bfloat16)
        result = jnp.einsum(
            "hqk,khd->qhd", probabilities, values_all, preferred_element_type=jnp.float32
        )
        return (result.astype(jnp.bfloat16), highest + jnp.log(totals))

    result, log_total = lax.map(one_block, blocks)
    return (result.reshape(length, head_count * head_width), log_total)


def attend_back(queries, keys_all, values_all, grad_heads, log_total, block_rows, factor):
    length, head_count, head_width = queries.shape
    block_count = length // block_rows
    query_blocks = queries.reshape(block_count, block_rows, head_count, head_width)
    grad_blocks = grad_heads.reshape(block_count, block_rows, head_count, head_width)

    def one_step(running, inputs):
        grad_keys, grad_values = running
        query_block, grad_block, log_block = inputs
        scores = (
            jnp.einsum("qhd,khd->hqk", query_block, keys_all, preferred_element_type=jnp.float32)
            * factor
        )
        probabilities = jnp.exp(scores - log_block)
        grad_values = grad_values + jnp.einsum(
            "hqk,qhd->khd",
            probabilities.astype(jnp.bfloat16),
            grad_block,
            preferred_element_type=jnp.float32,
        )
        grad_probs = jnp.einsum(
            "qhd,khd->hqk", grad_block, values_all, preferred_element_type=jnp.float32
        )
        centred = grad_probs - jnp.sum(probabilities * grad_probs, axis=-1, keepdims=True)
        grad_scores = (probabilities * centred).astype(jnp.bfloat16)
        grad_query = (
            jnp.einsum("hqk,khd->qhd", grad_scores, keys_all, preferred_element_type=jnp.float32)
            * factor
        )
        grad_keys = (
            grad_keys
            + jnp.einsum(
                "hqk,qhd->khd", grad_scores, query_block, preferred_element_type=jnp.float32
            )
            * factor
        )
        return ((grad_keys, grad_values), grad_query)

    empty_keys = jnp.zeros(keys_all.shape, jnp.float32)
    (grad_keys, grad_values), grad_query = lax.scan(
        one_step, (empty_keys, empty_keys), (query_blocks, grad_blocks, log_total)
    )
    flat = (length, head_count * head_width)
    return (grad_query.reshape(flat), grad_keys.reshape(flat), grad_values.reshape(flat))


def latent_pass(weights, tokens_in, cond_in, grad_out):
    (
        mod_weight,
        mod_bias,
        qkv_weight,
        qv_bias,
        out_weight,
        out_bias,
        up_weight,
        up_bias,
        down_weight,
        down_bias,
    ) = weights
    model_width = tokens_in.shape[1]
    tokens_here = tokens_in.shape[0]
    seq_count = lax.axis_size("seq")
    length = tokens_here * seq_count
    local_heads = H // seq_count
    block_rows = min(512, length)
    factor = HD ** (-0.5)
    cond_value = cond_in.astype(jnp.float32)
    cond_low = jax.nn.silu(cond_value).astype(jnp.bfloat16)
    modulation = matmul(cond_low[None, :], mod_weight)[0] + mod_bias.astype(jnp.float32)
    shift_one, scale_one, gate_one, shift_two, scale_two, gate_two = jnp.split(modulation, 6)
    inputs = tokens_in.astype(jnp.float32)
    normed_one = normalize(inputs)
    attn_in = (normed_one * (1.0 + scale_one) + shift_one).astype(jnp.bfloat16)
    qkv_bias = jnp.concatenate(
        [qv_bias[:model_width], jnp.zeros((model_width,), jnp.bfloat16), qv_bias[model_width:]]
    ).astype(jnp.float32)
    projected = (matmul(attn_in, qkv_weight) + qkv_bias).astype(jnp.bfloat16)
    queries = projected[:, :model_width]
    keys_all = projected[:, model_width : 2 * model_width]
    values_all = projected[:, 2 * model_width :]
    head_q, head_k, head_v = (
        lax.all_to_all(queries, "seq", split_axis=1, concat_axis=0, tiled=True),
        lax.all_to_all(keys_all, "seq", split_axis=1, concat_axis=0, tiled=True),
        lax.all_to_all(values_all, "seq", split_axis=1, concat_axis=0, tiled=True),
    )
    shaped = (length, local_heads, HD)
    head_q = head_q.reshape(shaped)
    head_k = head_k.reshape(shaped)
    head_v = head_v.reshape(shaped)
    heads_out, log_total = attend(head_q, head_k, head_v, block_rows, factor)
    back_tokens = lax.all_to_all(heads_out, "seq", split_axis=0, concat_axis=1, tiled=True)
    attn_branch = matmul(back_tokens, out_weight) + out_bias.astype(jnp.float32)
    middle = inputs + gate_one * attn_branch
    normed_two = normalize(middle)
    mlp_in = (normed_two * (1.0 + scale_two) + shift_two).astype(jnp.bfloat16)
    pre_act = matmul(mlp_in, up_weight) + up_bias.astype(jnp.float32)
    activated = jax.nn.gelu(pre_act, approximate=True).astype(jnp.bfloat16)
    mlp_branch = matmul(activated, down_weight) + down_bias.astype(jnp.float32)
    mixed_row = (middle + gate_two * mlp_branch).astype(jnp.bfloat16)
    grad_y = grad_out.astype(jnp.float32)
    grad_gate_two = jnp.sum(grad_y * mlp_branch, axis=0)
    grad_mlp = (gate_two * grad_y).astype(jnp.bfloat16)
    grad_down_weight = left_inner(activated, grad_mlp)
    grad_down_bias = jnp.sum(grad_mlp.astype(jnp.float32), axis=0)
    grad_act = right_inner(grad_mlp, down_weight)
    _, gelu_pull = jax.vjp(lambda argument: jax.nn.gelu(argument, approximate=True), pre_act)
    grad_pre = gelu_pull(grad_act)[0].astype(jnp.bfloat16)
    grad_up_weight = left_inner(mlp_in, grad_pre)
    grad_up_bias = jnp.sum(grad_pre.astype(jnp.float32), axis=0)
    grad_mlp_in = right_inner(grad_pre, up_weight)
    grad_shift_two = jnp.sum(grad_mlp_in, axis=0)
    grad_scale_two = jnp.sum(grad_mlp_in * normed_two, axis=0)
    _, second_pull = jax.vjp(normalize, middle)
    grad_middle = grad_y + second_pull(grad_mlp_in * (1.0 + scale_two))[0]
    grad_gate_one = jnp.sum(grad_middle * attn_branch, axis=0)
    grad_attn = (gate_one * grad_middle).astype(jnp.bfloat16)
    grad_out_weight = left_inner(back_tokens, grad_attn)
    grad_out_bias = jnp.sum(grad_attn.astype(jnp.float32), axis=0)
    grad_heads = right_inner(grad_attn, out_weight).astype(jnp.bfloat16)
    grad_heads_here = lax.all_to_all(
        grad_heads, "seq", split_axis=1, concat_axis=0, tiled=True
    ).reshape(shaped)
    grad_query, grad_keys, grad_values = attend_back(
        head_q, head_k, head_v, grad_heads_here, log_total, block_rows, factor
    )
    back_query, back_keys, back_values = (
        lax.all_to_all(
            grad_query.astype(jnp.bfloat16), "seq", split_axis=0, concat_axis=1, tiled=True
        ),
        lax.all_to_all(
            grad_keys.astype(jnp.bfloat16), "seq", split_axis=0, concat_axis=1, tiled=True
        ),
        lax.all_to_all(
            grad_values.astype(jnp.bfloat16), "seq", split_axis=0, concat_axis=1, tiled=True
        ),
    )
    grad_qkv = jnp.concatenate([back_query, back_keys, back_values], axis=1)
    grad_qkv_weight = left_inner(attn_in, grad_qkv)
    column_sums = jnp.sum(grad_qkv.astype(jnp.float32), axis=0)
    grad_qv_bias = jnp.concatenate([column_sums[:model_width], column_sums[2 * model_width :]])
    grad_attn_in = right_inner(grad_qkv, qkv_weight)
    grad_shift_one = jnp.sum(grad_attn_in, axis=0)
    grad_scale_one = jnp.sum(grad_attn_in * normed_one, axis=0)
    _, first_pull = jax.vjp(normalize, inputs)
    grad_tokens = grad_middle + first_pull(grad_attn_in * (1.0 + scale_one))[0]
    partial_mod = jnp.concatenate(
        [
            grad_shift_one,
            grad_scale_one,
            grad_gate_one,
            grad_shift_two,
            grad_scale_two,
            grad_gate_two,
        ]
    )
    summed_mod = lax.psum(partial_mod, "seq")
    grad_mod = summed_mod.astype(jnp.bfloat16)
    grad_low = right_inner(grad_mod[None, :], mod_weight)[0]
    _, silu_pull = jax.vjp(jax.nn.silu, cond_value)
    grad_cond = silu_pull(grad_low)[0]
    grads = (
        grad_qkv_weight,
        grad_qv_bias,
        grad_out_weight,
        grad_out_bias,
        grad_up_weight,
        grad_up_bias,
        grad_down_weight,
        grad_down_bias,
    )
    return (mixed_row, grad_tokens, grad_cond, grad_mod, cond_low, grads)


def per_device(
    latents,
    condition,
    mod_weight,
    mod_bias,
    qkv_weight,
    qv_bias,
    out_weight,
    out_bias,
    up_weight,
    up_bias,
    down_weight,
    down_bias,
    cotangent,
):
    micros = latents.shape[0]
    mixed_rows = []
    token_grads = []
    cond_grads = []
    mod_terms = None
    shares = None
    for latent_index in range(micros):
        weights = (
            lax.all_gather(mod_weight, "fsdp", axis=0, tiled=True),
            lax.all_gather(mod_bias, "fsdp", axis=0, tiled=True),
            lax.all_gather(qkv_weight, "fsdp", axis=0, tiled=True),
            lax.all_gather(qv_bias, "fsdp", axis=0, tiled=True),
            lax.all_gather(out_weight, "fsdp", axis=0, tiled=True),
            lax.all_gather(out_bias, "fsdp", axis=0, tiled=True),
            lax.all_gather(up_weight, "fsdp", axis=0, tiled=True),
            lax.all_gather(up_bias, "fsdp", axis=0, tiled=True),
            lax.all_gather(down_weight, "fsdp", axis=0, tiled=True),
            lax.all_gather(down_bias, "fsdp", axis=0, tiled=True),
        )
        mixed_row, grad_tokens, grad_cond, grad_mod, cond_low, grads = latent_pass(
            weights, latents[latent_index], condition[latent_index], cotangent[latent_index]
        )
        mixed_rows.append(mixed_row)
        token_grads.append(grad_tokens)
        cond_grads.append(grad_cond)
        term = (left_inner(cond_low[None, :], grad_mod[None, :]), grad_mod.astype(jnp.float32))
        mod_terms = term if mod_terms is None else jax.tree.map(jnp.add, mod_terms, term)
        part_qw, part_qb, part_ow, part_ob, part_uw, part_ub, part_dw, part_db = grads
        portion = (
            lax.psum_scatter(part_qw, ("fsdp", "seq"), scatter_dimension=0, tiled=True),
            lax.psum_scatter(part_qb, ("fsdp", "seq"), scatter_dimension=0, tiled=True),
            lax.psum_scatter(part_ow, ("fsdp", "seq"), scatter_dimension=0, tiled=True),
            lax.psum_scatter(part_ob, ("fsdp", "seq"), scatter_dimension=0, tiled=True),
            lax.psum_scatter(part_uw, ("fsdp", "seq"), scatter_dimension=0, tiled=True),
            lax.psum_scatter(part_ub, ("fsdp", "seq"), scatter_dimension=0, tiled=True),
            lax.psum_scatter(part_dw, ("fsdp", "seq"), scatter_dimension=0, tiled=True),
            lax.psum_scatter(part_db, ("fsdp", "seq"), scatter_dimension=0, tiled=True),
        )
        shares = portion if shares is None else jax.tree.map(jnp.add, shares, portion)
    term_weight, term_bias = mod_terms
    share_mw, share_mb = (
        lax.psum_scatter(
            term_weight.astype(jnp.bfloat16), "fsdp", scatter_dimension=0, tiled=True
        ).astype(jnp.float32),
        lax.psum_scatter(
            term_bias.astype(jnp.bfloat16), "fsdp", scatter_dimension=0, tiled=True
        ).astype(jnp.float32),
    )
    share_qw, share_qb, share_ow, share_ob, share_uw, share_ub, share_dw, share_db = shares
    summed = (
        lax.all_gather(share_qw.astype(jnp.bfloat16), "seq", axis=0, tiled=True).astype(
            share_qw.dtype
        ),
        lax.all_gather(share_qb.astype(jnp.bfloat16), "seq", axis=0, tiled=True).astype(
            share_qb.dtype
        ),
        lax.all_gather(share_ow.astype(jnp.bfloat16), "seq", axis=0, tiled=True).astype(
            share_ow.dtype
        ),
        lax.all_gather(share_ob.astype(jnp.bfloat16), "seq", axis=0, tiled=True).astype(
            share_ob.dtype
        ),
        lax.all_gather(share_uw.astype(jnp.bfloat16), "seq", axis=0, tiled=True).astype(
            share_uw.dtype
        ),
        lax.all_gather(share_ub.astype(jnp.bfloat16), "seq", axis=0, tiled=True).astype(
            share_ub.dtype
        ),
        lax.all_gather(share_dw.astype(jnp.bfloat16), "seq", axis=0, tiled=True).astype(
            share_dw.dtype
        ),
        lax.all_gather(share_db.astype(jnp.bfloat16), "seq", axis=0, tiled=True).astype(
            share_db.dtype
        ),
    )
    return (
        jnp.stack(mixed_rows),
        jnp.stack(token_grads),
        jnp.stack(cond_grads),
        share_mw,
        share_mb,
        summed[0],
        summed[1],
        summed[2],
        summed[3],
        summed[4],
        summed[5],
        summed[6],
        summed[7],
    )


def solution(mesh):
    in_specs = (
        P("fsdp", "seq", None),
        P("fsdp", None),
        P("fsdp", None),
        P("fsdp"),
        P("fsdp", None),
        P("fsdp"),
        P("fsdp", None),
        P("fsdp"),
        P("fsdp", None),
        P("fsdp"),
        P("fsdp", None),
        P("fsdp"),
        P("fsdp", "seq", None),
    )
    out_specs = (
        P("fsdp", "seq", None),
        P("fsdp", "seq", None),
        P("fsdp", None),
        P("fsdp", None),
        P("fsdp"),
        P("fsdp", None),
        P("fsdp"),
        P("fsdp", None),
        P("fsdp"),
        P("fsdp", None),
        P("fsdp"),
        P("fsdp", None),
        P("fsdp"),
    )
    return jax.shard_map(
        per_device, mesh=mesh, in_specs=in_specs, out_specs=out_specs, check_vma=False
    )
```

profile of v0, /device:TPU:0, one launch (start us, length us, event | category | flops | bytes accessed | tf_op | source)
XLA Modules:
  0.0 1995.7 jit_solution(13347989620852579815)
XLA Ops:
  15.1 41.5 %all-reduce.22 = (bf16[2304]{0:T(1024)(128)(2,1)S(1)}, bf16[6912]{0:T(1024)(128)(2,1)S(1)}, bf16[4608]{0:T(1024)(128)(2,1)S(1)}, bf16[1152]{0:T(1024)(128)(2,1)S(1)}, bf16[1152]{0:T(1024)(128)(2,1)}) all-reduce(bf16[2304]{0:T(1024)(128)(2,1)S(1)} %dynamic-update-slice.1, ...), channel_id=1, replica_groups=mesh['fsdp'=8,'seq'=4] {'fsdp'}, use_global_device_ids=true, to_apply=%add.1 | all-reduce | flops 16128 | bytes 64512
  57.6 173.7 %all-gather.11.cloned.1.call-done = bf16[1152,6912]{1,0:T(8,128)(2,1)} async-done(((bf16[144,6912]{1,0:T(8,128)(2,1)}), bf16[1152,6912]{1,0:T(8,128)(2,1)}) %all-gather.11.cloned.1.call-update) | async-done | bytes 15925264 | tf_op jit(solution)/shard_map/all_gather | solution.py:250
  231.3 7.9 convolution_reduce_fusion.1
  245.1 106.1 %all-gather.13.cloned.1.call-done = bf16[1152,3456]{1,0:T(8,128)(2,1)} async-done(((bf16[144,3456]{1,0:T(8,128)(2,1)}), bf16[1152,3456]{1,0:T(8,128)(2,1)}) %all-gather.13.cloned.1.call-update) | async-done | bytes 7962640 | tf_op jit(solution)/shard_map/all_gather | solution.py:252
  395.4 11.3 all-gather.15.cloned.1.call-done
  410.2 149.6 %all-gather.17.cloned.1.call-done = bf16[1152,4608]{1,0:T(8,128)(2,1)} async-done(((bf16[144,4608]{1,0:T(8,128)(2,1)}), bf16[1152,4608]{1,0:T(8,128)(2,1)}) %all-gather.17.cloned.1.call-update) | async-done | bytes 10616848 | tf_op jit(solution)/shard_map/all_gather | solution.py:256
  565.6 146.9 %all-gather.19.cloned.1.call-done = bf16[4608,1152]{1,0:T(8,128)(2,1)} async-done(((bf16[576,1152]{1,0:T(8,128)(2,1)}), bf16[4608,1152]{1,0:T(8,128)(2,1)}) %all-gather.19.cloned.1.call-update) | async-done | bytes 10616848 | tf_op jit(solution)/shard_map/all_gather | solution.py:258
  712.5 8.8 convert_reduce_fusion.1
  785.9 7.3 fusion.80
  845.7 12.0 fusion.96
  868.3 13.6 convolution_add_fusion
  889.8 10.9 fusion.128
  901.3 10.9 fusion.120
  912.8 10.9 convert_reduce_fusion
  929.8 6.8 convolution_add_fusion.10
  947.9 17.9 convolution_add_fusion.1
  1004.4 14.0 convolution_add_fusion.2
  1018.4 545.7 %fusion.129 = (f32[48,3456]{1,0:T(8,128)S(1)}, f32[48,1152]{1,0:T(8,128)}, f32[40,4608]{1,0:T(8,128)S(1)}) fusion(f32[1152,3456]{1,0:T(8,128)} %convolution_add_fusion.2, f32[1152,1152]{1,0:T(8,128)} %convolution_add_fusion.3, f32[1152,4608]{1,0:T(8,128)} %convolution_add_fusion.1), kind=kCustom, calls=%all-reduce-scatter.3 | all-reduce-scatter fusion | flops 12976130 | bytes 44089344
  1564.1 15.7 collective-permute-start.18
  1579.8 13.4 collective-permute-start.17
  1597.7 7.5 fusion.78
  1608.2 16.8 concatenate.38
  1632.5 11.8 all-reduce.21
  1680.1 9.9 convolution_reduce_fusion.2
  1692.2 9.8 convolution_reduce_fusion.3
  1709.9 7.0 collective-permute-start.10
  1717.0 56.5 %all-reduce.20 = (bf16[2304]{0:T(1024)(128)(2,1)S(1)}, bf16[1152]{0:T(1024)(128)(2,1)S(1)}, bf16[4608]{0:T(1024)(128)(2,1)S(1)}, bf16[1152]{0:T(1024)(128)(2,1)S(1)}) all-reduce(f32[2304]{0:T(1024)S(1)} %maximum_add_fusion, f32[1152]{0:T(1024)S(1)} %add.377, ...), channel_id=13, replica_groups=mesh['fsdp'=8,'seq'=4] {'fsdp','seq'}, use_global_device_ids=true, to_apply=%region_41.42.clone | all-reduce | flops 9216 | bytes 55296
  1783.0 38.5 %all-reduce.9 = bf16[6912]{0:T(1024)(128)(2,1)S(1)} all-reduce(bf16[6912]{0:T(1024)(128)(2,1)S(1)} %add_convert_fusion.5), channel_id=11, replica_groups=mesh['fsdp'=8,'seq'=4] {'fsdp'}, use_global_device_ids=true, to_apply=%region_37.38.clone | all-reduce | flops 6912 | bytes 27648
  1848.5 13.5 all-gather.1
  1862.9 33.2 %concatenate.36 = bf16[420,3456]{1,0:T(8,128)(2,1)} concatenate(bf16[36,3456]{1,0:T(8,128)(2,1)} %copy-done.59, bf16[48,3456]{1,0:T(8,128)(2,1)} %collective-permute-done.6, bf16[48,3456]{1,0:T(8,128)(2,1)} %collective-permute-done.5, bf16[48,3456]{1,0:T(8,128)(2,1)S(1)} %collective-permute-done.4, bf16[48,3456]{1,0:T(8,128)(2,1)S(1)} %collective-permute-done.3, ...), dimensions={0} | concatenate | bytes 6137856
  1897.1 13.5 all-gather
  1917.9 67.2 %reduce-scatter.9.cloned.1.call-done = bf16[144,6912]{1,0:T(8,128)(2,1)} async-done(((bf16[1152,6912]{1,0:T(8,128)(2,1)}), bf16[144,6912]{1,0:T(8,128)(2,1)}) %reduce-scatter.9.cloned.1.call-update) | async-done | bytes 1990672 | tf_op jit(solution)/shard_map/reduce_scatter | solution.py:283
  (606 shorter events, 363.9 us)
Async XLA Ops:
  7.2 224.1 %all-gather.11.cloned.1.call-start = ((), (), s32[]{:S(2)}) async-start(), calls=%async_computation.18 | async-start | bytes 17915904 | tf_op jit(solution)/shard_map/all_gather | solution.py:250
  8.0 343.3 %all-gather.13.cloned.1.call-start = ((), (), s32[]{:S(2)}) async-start(), calls=%async_computation.19 | async-start | bytes 8957952 | tf_op jit(solution)/shard_map/all_gather | solution.py:252
  8.8 397.9 %all-gather.15.cloned.1.call-start = ((), (), s32[]{:S(2)}) async-start(), calls=%async_computation.20 | async-start | bytes 2985984 | tf_op jit(solution)/shard_map/all_gather | solution.py:254
  9.5 550.3 %all-gather.17.cloned.1.call-start = ((), (), s32[]{:S(2)}) async-start(), calls=%async_computation.21 | async-start | bytes 11943936 | tf_op jit(solution)/shard_map/all_gather | solution.py:256
  10.1 702.4 %all-gather.19.cloned.1.call-start = ((), (), s32[]{:S(2)}) async-start(), calls=%async_computation.22 | async-start | bytes 11943936 | tf_op jit(solution)/shard_map/all_gather | solution.py:258
  391.9 14.8 all-to-all-start.3
  751.3 12.7 all-to-all-start.11
  841.4 16.3 all-to-all-start.7
  845.5 798.9 %reduce-scatter.11.cloned.1.call-start = ((), (), s32[]{:S(2)}) async-start(), calls=%async_computation.25 | async-start | bytes 21897216 | tf_op jit(solution)/shard_map/reduce_scatter | solution.py:277
  944.5 21.4 %all-to-all-start.12 = ((bf16[128,4,288]{0,2,1:T(8,128)(2,1)}), bf16[128,4,288]{0,2,1:T(8,128)(2,1)S(1)}, u32[]{:S(2)}, u32[]{:S(2)}) async-start(bf16[128,4,288]{0,2,1:T(8,128)(2,1)} %bitcast.42), calls=%async_computation.12 | async-start | bytes 589824 | tf_op jit(solution)/shard_map/all_to_all | solution.py:173
  970.3 11.2 all-to-all-start.15
  991.4 13.0 all-to-all-start.13
  994.9 917.1 %all-gather.23.cloned.1.call-start = ((), (), s32[]{:S(2)}) async-start(), calls=%async_computation.26 | async-start | bytes 1843200 | tf_op jit(solution)/shard_map/all_gather | solution.py:304
  1564.1 43.3 %collective-permute-start.18 = (bf16[40,4608]{1,0:T(8,128)(2,1)S(1)}, bf16[40,4608]{1,0:T(8,128)(2,1)}, u32[]{:S(2)}, u32[]{:S(2)}) collective-permute-start(bf16[40,4608]{1,0:T(8,128)(2,1)S(1)} %convert.102), channel_id=1, source_target_pairs={{0,3},{1,4},{2,5},{3,6},{4,7},{5,8},{6,9},{7,10},{8,11},{9,12},{10... | collective-permute-start | bytes 1105928
  1579.8 27.7 %collective-permute-start.17 = (bf16[40,4608]{1,0:T(8,128)(2,1)S(1)}, bf16[40,4608]{1,0:T(8,128)(2,1)S(1)}, u32[]{:S(2)}, u32[]{:S(2)}) collective-permute-start(bf16[40,4608]{1,0:T(8,128)(2,1)S(1)} %convert.102), channel_id=1, source_target_pairs={{0,2},{1,3},{2,4},{3,5},{4,6},{5,7},{6,8},{7,9},{8,10},{9,11},{10,... | collective-permute-start | bytes 1105928
  1593.2 15.0 collective-permute-start.16
  1596.3 11.1 collective-permute-start.19
  1627.0 287.7 %all-gather.21.cloned.1.call-start = ((), (), s32[]{:S(2)}) async-start(), calls=%async_computation.24 | async-start | bytes 1658880 | tf_op jit(solution)/shard_map/all_gather | solution.py:310
  1646.3 338.8 %reduce-scatter.9.cloned.1.call-start = ((), (), s32[]{:S(2)}) async-start(), calls=%async_computation.23 | async-start | bytes 17915904 | tf_op jit(solution)/shard_map/reduce_scatter | solution.py:283
  1661.5 181.0 %collective-permute-start.6 = (bf16[48,3456]{1,0:T(8,128)(2,1)}, bf16[48,3456]{1,0:T(8,128)(2,1)}, u32[]{:S(2)}, u32[]{:S(2)}) collective-permute-start(bf16[48,3456]{1,0:T(8,128)(2,1)} %convert.103), channel_id=1, source_target_pairs={{0,7},{1,8},{2,9},{3,10},{4,11},{5,12},{6,13},{7,14},{8,15},{9,16}... | collective-permute-start | bytes 995336
  1665.9 180.3 %collective-permute-start.5 = (bf16[48,3456]{1,0:T(8,128)(2,1)}, bf16[48,3456]{1,0:T(8,128)(2,1)}, u32[]{:S(2)}, u32[]{:S(2)}) collective-permute-start(bf16[48,3456]{1,0:T(8,128)(2,1)} %convert.103), channel_id=1, source_target_pairs={{0,6},{1,7},{2,8},{3,9},{4,10},{5,11},{6,12},{7,13},{8,14},{9,15},... | collective-permute-start | bytes 995336
  1670.0 34.1 %collective-permute-start.14 = (bf16[48,1152]{1,0:T(8,128)(2,1)S(1)}, bf16[48,1152]{1,0:T(8,128)(2,1)S(1)}, u32[]{:S(2)}, u32[]{:S(2)}) collective-permute-start(bf16[48,1152]{1,0:T(8,128)(2,1)S(1)} %convert.104), channel_id=1, source_target_pairs={{0,7},{1,8},{2,9},{3,10},{4,11},{5,12},{6,13},{7,14},{8,15},{9,16}... | collective-permute-start | bytes 331784
  1671.8 35.4 %collective-permute-start.13 = (bf16[48,1152]{1,0:T(8,128)(2,1)S(1)}, bf16[48,1152]{1,0:T(8,128)(2,1)S(1)}, u32[]{:S(2)}, u32[]{:S(2)}) collective-permute-start(bf16[48,1152]{1,0:T(8,128)(2,1)S(1)} %convert.104), channel_id=1, source_target_pairs={{0,6},{1,7},{2,8},{3,9},{4,10},{5,11},{6,12},{7,13},{8,14},{9,15},... | collective-permute-start | bytes 331784
  1677.8 24.2 %collective-permute-start.15 = (bf16[36,1152]{1,0:T(8,128)(2,1)S(1)}, bf16[36,1152]{1,0:T(8,128)(2,1)S(1)}, u32[]{:S(2)}, u32[]{:S(2)}) collective-permute-start(bf16[36,1152]{1,0:T(8,128)(2,1)S(1)} %slice.87), channel_id=1, source_target_pairs={{0,8},{1,9},{2,10},{3,11},{4,12},{5,13},{6,14},{7,15},{8,16},{9,17... | collective-permute-start | bytes 248840
  1704.1 133.0 %collective-permute-start.7 = (bf16[36,3456]{1,0:T(8,128)(2,1)}, bf16[36,3456]{1,0:T(8,128)(2,1)S(1)}, u32[]{:S(2)}, u32[]{:S(2)}) collective-permute-start(bf16[36,3456]{1,0:T(8,128)(2,1)} %slice.86), channel_id=1, source_target_pairs={{0,8},{1,9},{2,10},{3,11},{4,12},{5,13},{6,14},{7,15},{8,16},{9,17... | collective-permute-start | bytes 746504
  1707.2 114.2 %collective-permute-start.11 = (bf16[48,1152]{1,0:T(8,128)(2,1)S(1)}, bf16[48,1152]{1,0:T(8,128)(2,1)S(1)}, u32[]{:S(2)}, u32[]{:S(2)}) collective-permute-start(bf16[48,1152]{1,0:T(8,128)(2,1)S(1)} %convert.104), channel_id=1, source_target_pairs={{0,4},{1,5},{2,6},{3,7},{4,8},{5,9},{6,10},{7,11},{8,12},{9,13},{1... | collective-permute-start | bytes 331784
  1709.9 115.2 %collective-permute-start.10 = (bf16[48,1152]{1,0:T(8,128)(2,1)S(1)}, bf16[48,1152]{1,0:T(8,128)(2,1)S(1)}, u32[]{:S(2)}, u32[]{:S(2)}) collective-permute-start(bf16[48,1152]{1,0:T(8,128)(2,1)S(1)} %convert.104), channel_id=1, source_target_pairs={{0,3},{1,4},{2,5},{3,6},{4,7},{5,8},{6,9},{7,10},{8,11},{9,12},{10... | collective-permute-start | bytes 331784
  1827.7 35.1 %collective-permute-start.4 = (bf16[48,3456]{1,0:T(8,128)(2,1)}, bf16[48,3456]{1,0:T(8,128)(2,1)S(1)}, u32[]{:S(2)}, u32[]{:S(2)}) collective-permute-start(bf16[48,3456]{1,0:T(8,128)(2,1)} %convert.103), channel_id=1, source_target_pairs={{0,5},{1,6},{2,7},{3,8},{4,9},{5,10},{6,11},{7,12},{8,13},{9,14},{... | collective-permute-start | bytes 995336
  1829.1 33.7 %collective-permute-start.3 = (bf16[48,3456]{1,0:T(8,128)(2,1)}, bf16[48,3456]{1,0:T(8,128)(2,1)S(1)}, u32[]{:S(2)}, u32[]{:S(2)}) collective-permute-start(bf16[48,3456]{1,0:T(8,128)(2,1)} %convert.103), channel_id=1, source_target_pairs={{0,4},{1,5},{2,6},{3,7},{4,8},{5,9},{6,10},{7,11},{8,12},{9,13},{1... | collective-permute-start | bytes 995336
  1837.1 25.7 %collective-permute-start.2 = (bf16[48,3456]{1,0:T(8,128)(2,1)}, bf16[48,3456]{1,0:T(8,128)(2,1)S(1)}, u32[]{:S(2)}, u32[]{:S(2)}) collective-permute-start(bf16[48,3456]{1,0:T(8,128)(2,1)} %convert.103), channel_id=1, source_target_pairs={{0,3},{1,4},{2,5},{3,6},{4,7},{5,8},{6,9},{7,10},{8,11},{9,12},{10... | collective-permute-start | bytes 995336
  1842.5 20.4 %collective-permute-start.1 = (bf16[48,3456]{1,0:T(8,128)(2,1)}, bf16[48,3456]{1,0:T(8,128)(2,1)}, u32[]{:S(2)}, u32[]{:S(2)}) collective-permute-start(bf16[48,3456]{1,0:T(8,128)(2,1)} %convert.103), channel_id=1, source_target_pairs={{0,2},{1,3},{2,4},{3,5},{4,6},{5,7},{6,8},{7,9},{8,10},{9,11},{10,... | collective-permute-start | bytes 995336
  1846.1 16.7 collective-permute-start
  (174 other events, 8638.7 us)
Sparse Core Ops, SparseCore 0:
  10.2 221.0 all-gather.10
  233.5 117.7 all-gather.12
  353.4 53.2 all-gather.14
  408.7 151.0 all-gather.16
  561.8 150.6 all-gather.18
  882.0 284.0 reduce-scatter.10
  1627.1 21.1 all-gather.22
  1650.0 18.2 all-gather.20
  1672.7 312.2 reduce-scatter.8
where the time goes:
time: 2010 us; the launch traced here: 2000 us
  blocking collectives  727 us (36%)
  waiting for transfers between devices  707 us (35%)
  matrix products  228 us (11%)
  starting transfers between devices  147 us (7%)
  local copies, waits for them, and re-layouts  117 us (6%)
  other arithmetic  47.4 us (2%)
  between operations  22.1 us (1%)
    unnamed x5, blocking collectives  688 us
    all_gather x1, waiting for transfers between devices, per_device(): lax.all_gather(mod_weight, 'fsdp', axis=0, tiled=True)  174 us
    all_gather x1, waiting for transfers between devices, per_device(): lax.all_gather(up_weight, 'fsdp', axis=0, tiled=True)  150 us
    all_gather x1, waiting for transfers between devices, per_device(): lax.all_gather(down_weight, 'fsdp', axis=0, tiled=True)  147 us
    all_gather x1, waiting for transfers between devices, per_device(): lax.all_gather(qkv_weight, 'fsdp', axis=0, tiled=True)  106 us
    dot_general x8, matrix products, left_inner(): lax.dot_general(left_side, right_side, (((0,), (0,)), ((), ())), preferre...  89.7 us
    unnamed x20, starting transfers between devices  87.6 us
    unnamed x363, local copies, waits for them, and re-layouts  78.1 us
  transfers between devices with their start and end apart: 45, of which 18 were waited for; matrix products, arithmetic and copies ran while one was open for 42% of the time, Pallas kernels for 0%

commit v1 on v0

v1 whole, which is shorter than its diff:
```python
import jax
import jax.numpy as jnp
from jax import lax
from jax.sharding import PartitionSpec as P

H = 16
HD = 72
GELU_ROOT = (2.0 / 3.141592653589793) ** 0.5
GELU_CUBE = 0.044715


def matmul(left_side, right_side):
    return jnp.dot(left_side, right_side, preferred_element_type=jnp.float32)


def contract(left_side, right_side, left_dim, right_dim):
    return lax.dot_general(
        left_side,
        right_side,
        (((left_dim,), (right_dim,)), ((), ())),
        preferred_element_type=jnp.float32,
    )


def low(values):
    return values.astype(jnp.bfloat16)


def wide(values):
    return values.astype(jnp.float32)


def normalize(values):
    centre = values - jnp.mean(values, axis=-1, keepdims=True)
    spread = jnp.mean(centre * centre, axis=-1, keepdims=True)
    inverse = lax.rsqrt(spread + 1e-06)
    return centre * inverse, inverse


def normalize_back(normed, inverse, grad):
    inner = jnp.mean(grad * normed, axis=-1, keepdims=True)
    return (grad - jnp.mean(grad, axis=-1, keepdims=True) - normed * inner) * inverse


def pick(values, index, axis):
    return lax.dynamic_index_in_dim(values, index, axis, keepdims=False)


def ordered(first, mine, other, axis):
    return jnp.where(
        first, jnp.concatenate([mine, other], axis), jnp.concatenate([other, mine], axis)
    )


class Place:
    def __init__(self):
        self.shards = lax.axis_size("fsdp")
        self.seats = lax.axis_size("seq")
        self.line_size = self.shards // 2
        self.shard = lax.axis_index("fsdp")
        self.seat = lax.axis_index("seq")
        self.line = self.shard // 2
        self.pair = self.shard % 2
        self.side = self.seat // 2
        self.core = self.seat % 2

    def to_core(self, values):
        return lax.ppermute(values, "seq", [(i, i ^ 1) for i in range(self.seats)])

    def to_side(self, values):
        return lax.ppermute(values, "seq", [(i, i ^ 2) for i in range(self.seats)])

    def to_pair(self, values):
        return lax.ppermute(values, "fsdp", [(i, i ^ 1) for i in range(self.shards)])

    def to_line(self, values):
        return lax.ppermute(
            values, "fsdp", [(i, (i + 2) % self.shards) for i in range(self.shards)]
        )

    def spread(self, tokens):
        count = tokens.shape[0] // 2
        halves = tokens.reshape((2, count) + tokens.shape[1:])
        near = self.to_core(pick(halves, 1 - self.core, 0))
        both = jnp.concatenate([pick(halves, self.core, 0), near], axis=1)
        return jnp.concatenate([both, self.to_side(both)], axis=1)

    def unspread(self, mine):
        tokens = mine.shape[1] // 2
        near = self.to_core(mine[:, tokens:])
        return ordered(self.core == 0, mine[:, :tokens], near, 0)

    def gather(self, piece):
        total = jnp.zeros((self.shards,) + piece.shape, piece.dtype)
        for step in range(self.line_size):
            near = self.to_pair(piece)
            start = (self.line - step) % self.line_size * 2
            total = lax.dynamic_update_index_in_dim(total, piece, start + self.pair, 0)
            total = lax.dynamic_update_index_in_dim(total, near, start + 1 - self.pair, 0)
            if step + 1 < self.line_size:
                piece = self.to_line(piece)
        return total

    def reduce(self, mine, theirs):
        rows, columns = mine.shape
        met = self.to_core(low(theirs))
        total = low(mine + wide(met))
        blocks = total.reshape(self.line_size, 2, rows // self.shards, columns)
        got = self.to_pair(pick(blocks, 1 - self.pair, 1))
        kept = low(wide(pick(blocks, self.pair, 1)) + wide(got))
        run = None
        for step in range(1, self.line_size):
            block = pick(kept, (self.line - step) % self.line_size, 0)
            run = self.to_line(block if run is None else low(wide(block) + wide(run)))
        return low(wide(pick(kept, self.line, 0)) + wide(run))

    def share(self, quarter):
        half = self.to_side(quarter)
        sides = ordered(self.side == 0, quarter[None], half[None], 0)
        cores = self.to_core(sides)
        whole = ordered(self.core == 0, sides[:, None], cores[:, None], 1)
        return whole.reshape((4,) + quarter.shape)

    def exchange(self, values):
        return lax.all_to_all(values, "fsdp", split_axis=0, concat_axis=0, tiled=True)

    def to_all(self, values):
        return self.exchange(jnp.broadcast_to(values[None], (self.shards,) + values.shape))


def per_device(
    latents,
    condition,
    mod_weight,
    mod_bias,
    qkv_weight,
    qv_bias,
    out_weight,
    out_bias,
    up_weight,
    up_bias,
    down_weight,
    down_bias,
    cotangent,
):
    here = Place()
    shards, seat, side, core = here.shards, here.seat, here.side, here.core
    micros, tokens, width = latents.shape
    count = micros // 2
    length = 4 * tokens
    rows = width // shards
    hidden = up_weight.shape[1]
    heads = H // 4
    part = heads * HD
    factor = HD ** (-0.5)
    flat = (count * length, width)

    qkv_piece = pick(qkv_weight.reshape(rows, 3, 4, part), seat, 2).reshape(rows, 3 * part)
    block = hidden // shards // 4
    up_piece = pick(up_weight.reshape(rows, shards, 4, block), seat, 2).reshape(
        rows, shards * block
    )
    down_piece = pick(down_weight.reshape(4, block, width), seat, 0)
    out_piece = pick(out_weight.reshape(2, rows // 2, width), core, 0)

    qkv_mine = here.gather(qkv_piece).reshape(width, 3 * part)
    qkv_near = here.to_core(qkv_mine)

    small = jnp.concatenate(
        [condition.reshape(-1), mod_bias, qv_bias, out_bias, up_bias, down_bias]
    )
    small = here.to_all(small)
    cuts = [micros * width]
    for vector in (mod_bias, qv_bias, out_bias, up_bias):
        cuts.append(cuts[-1] + vector.shape[0])
    cond_all, mod_bias, qv_bias, out_bias, up_bias, down_bias = jnp.split(small, cuts, axis=1)
    mod_bias, qv_bias, out_bias, up_bias, down_bias = (
        wide(vector.reshape(-1)) for vector in (mod_bias, qv_bias, out_bias, up_bias, down_bias)
    )
    cond_all = cond_all.reshape(shards * micros, width)
    cond_low = low(jax.nn.silu(wide(cond_all)))
    cond_rows = lax.dynamic_slice_in_dim(cond_low, here.shard * rows, rows, 1)
    cond_mine = pick(cond_rows.reshape(shards, 2, count, rows), core, 1)
    mod_part = matmul(cond_mine.reshape(shards * count, rows), mod_weight)
    mod_part = here.exchange(mod_part.reshape(shards, count, 6 * width))
    modulation = jnp.sum(mod_part, axis=0) + mod_bias
    shift_one, scale_one, gate_one, shift_two, scale_two, gate_two = (
        vector[:, None] for vector in jnp.split(modulation, 6, axis=1)
    )

    inputs = wide(here.spread(latents))
    normed_one, inverse_one = normalize(inputs)
    attn_in = low(normed_one * (1.0 + scale_one) + shift_one).reshape(flat)

    qv_parts = jnp.concatenate([qv_bias[:width], jnp.zeros((width,), jnp.float32), qv_bias[width:]])
    qv_parts = qv_parts.reshape(3, 4, part)

    def project(weight, which):
        bias = pick(qv_parts, which, 1).reshape(3 * part, 1)
        values = low(contract(weight, attn_in, 0, 1) + bias)
        return values.reshape(3, heads, HD, count, length)

    def attend(values):
        queries, keys, contents = values
        scores = (
            jnp.einsum("hdbk,hdbq->hbkq", keys, queries, preferred_element_type=jnp.float32)
            * factor
        )
        raised = jnp.exp(scores - jnp.max(scores, axis=2, keepdims=True))
        probs = raised / jnp.sum(raised, axis=2, keepdims=True)
        result = jnp.einsum(
            "hdbk,hbkq->hdbq", contents, low(probs), preferred_element_type=jnp.float32
        )
        return probs, low(result).reshape(part, count * length)

    values_mine = project(qkv_mine, seat)
    probs_mine, result_mine = attend(values_mine)
    near_seat = seat + 1 - 2 * core
    values_near = project(qkv_near, near_seat)
    probs_near, result_near = attend(values_near)
    heads_half = ordered(core == 0, result_mine, result_near, 0)

    heads_far = here.to_side(heads_half).reshape(2 * part, count, 2, length // 2)
    heads_far = heads_far[:, :, ::-1].reshape(heads_half.shape)
    heads_out = ordered(side == 0, heads_half, heads_far, 0)

    out_mine = here.gather(out_piece)
    out_near = here.to_core(out_mine)
    out_full = ordered(core == 0, out_mine[:, None], out_near[:, None], 1).reshape(width, width)
    up_mine = here.gather(up_piece).reshape(width, shards * block)
    up_near = here.to_core(up_mine)
    down_mine = here.gather(down_piece).reshape(shards * block, width)
    down_near = here.to_core(down_mine)

    attn_branch = (contract(heads_out, out_full, 0, 0) + out_bias).reshape(inputs.shape)
    middle = inputs + gate_one * attn_branch
    normed_two, inverse_two = normalize(middle)
    mlp_in = low(normed_two * (1.0 + scale_two) + shift_two).reshape(flat)

    grad_y = wide(here.spread(cotangent))
    grad_mlp = low(gate_two * grad_y).reshape(flat)
    up_parts = up_bias.reshape(shards, 4, block)

    def feed(up, which):
        bias = pick(up_parts, which, 1).reshape(shards * block)
        pre_act = matmul(mlp_in, up) + bias
        squared = pre_act * pre_act
        bent = jnp.tanh(GELU_ROOT * pre_act * (1.0 + GELU_CUBE * squared))
        activated = low(0.5 * pre_act * (1.0 + bent))
        slope = 0.5 * (1.0 + bent) + 0.5 * GELU_ROOT * pre_act * (1.0 - bent * bent) * (
            1.0 + 3.0 * GELU_CUBE * squared
        )
        return activated, slope

    def feed_back(down, slope):
        return low(contract(grad_mlp, down, 1, 1) * slope)

    act_mine, slope_mine = feed(up_mine, seat)
    act_near, slope_near = feed(up_near, near_seat)
    pre_mine = feed_back(down_mine, slope_mine)
    pre_near = feed_back(down_near, slope_near)

    mlp_grad_part = low(contract(pre_mine, up_mine, 1, 1) + contract(pre_near, up_near, 1, 1))
    mlp_grad_far = here.to_side(mlp_grad_part).reshape(count, 2, length // 2, width)
    mlp_grad_far = mlp_grad_far[:, ::-1].reshape(inputs.shape)
    grad_mlp_in = wide(mlp_grad_part.reshape(inputs.shape)) + wide(mlp_grad_far)

    branch_part = matmul(act_mine, down_mine) + matmul(act_near, down_near)
    branch_part = branch_part.reshape(inputs.shape)
    own = length // 2
    branch_far = here.to_side(low(branch_part[:, own:]))
    mlp_branch = branch_part[:, :own] + wide(branch_far) + down_bias
    grad_gate_two = jnp.sum(grad_y[:, :own] * mlp_branch, axis=1)
    mixed = here.unspread(low(middle[:, :own] + gate_two * mlp_branch))

    grad_down = here.reduce(
        contract(act_mine, grad_mlp, 0, 0), contract(act_near, grad_mlp, 0, 0)
    )
    grad_up = here.reduce(contract(mlp_in, pre_mine, 0, 0), contract(mlp_in, pre_near, 0, 0))

    grad_shift_two = jnp.sum(grad_mlp_in[:, :own], axis=1)
    grad_scale_two = jnp.sum((grad_mlp_in * normed_two)[:, :own], axis=1)
    grad_middle = grad_y + normalize_back(
        normed_two, inverse_two, grad_mlp_in * (1.0 + scale_two)
    )
    grad_gate_one = jnp.sum((grad_middle * attn_branch)[:, :own], axis=1)
    grad_attn = low(gate_one * grad_middle).reshape(flat)

    out_half = lax.dynamic_slice_in_dim(out_full, side * 2 * part, 2 * part, 0)
    grad_heads = low(contract(out_half, grad_attn, 1, 1))
    grad_heads = grad_heads.reshape(2, heads, HD, count, length)
    grad_attn_cuts = grad_attn.reshape(count * length, 4, width // 4)
    grad_out = here.reduce(
        contract(heads_out, pick(grad_attn_cuts, seat, 1), 1, 0),
        contract(heads_out, pick(grad_attn_cuts, near_seat, 1), 1, 0),
    )

    def attend_back(values, probs, grad_result):
        queries, keys, contents = values
        grad_probs = jnp.einsum(
            "hdbk,hdbq->hbkq", contents, grad_result, preferred_element_type=jnp.float32
        )
        inner = jnp.sum(probs * grad_probs, axis=2, keepdims=True)
        grad_scores = low(probs * (grad_probs - inner))
        grad_queries = factor * jnp.einsum(
            "hdbk,hbkq->hdbq", keys, grad_scores, preferred_element_type=jnp.float32
        )
        grad_keys = factor * jnp.einsum(
            "hdbq,hbkq->hdbk", queries, grad_scores, preferred_element_type=jnp.float32
        )
        grad_contents = jnp.einsum(
            "hdbq,hbkq->hdbk", grad_result, low(probs), preferred_element_type=jnp.float32
        )
        grads = jnp.stack([low(grad_queries), low(grad_keys), low(grad_contents)])
        return grads.reshape(3 * part, count * length)

    qkv_grad_mine = attend_back(values_mine, probs_mine, pick(grad_heads, core, 0))
    qkv_grad_near = attend_back(values_near, probs_near, pick(grad_heads, 1 - core, 0))
    grad_qkv = here.reduce(
        contract(attn_in, qkv_grad_mine, 0, 1), contract(attn_in, qkv_grad_near, 0, 1)
    )
    attn_grad_part = contract(qkv_grad_mine, qkv_mine, 0, 1) + contract(
        qkv_grad_near, qkv_near, 0, 1
    )
    attn_grad_part = attn_grad_part.reshape(inputs.shape)
    part_shift = jnp.sum(attn_grad_part, axis=1)
    part_scale = jnp.sum(attn_grad_part * normed_one, axis=1)
    attn_grad_far = here.to_side(low(attn_grad_part[:, own:]))
    grad_attn_in = attn_grad_part[:, :own] + wide(attn_grad_far)
    grad_tokens = grad_middle[:, :own] + normalize_back(
        normed_one[:, :own], inverse_one[:, :own], grad_attn_in * (1.0 + scale_one)
    )
    grad_latents = here.unspread(grad_tokens)

    grad_mod = jnp.concatenate(
        [part_shift, part_scale, grad_gate_one, grad_shift_two, grad_scale_two, grad_gate_two],
        axis=1,
    )
    qv_sums = jnp.zeros((2, 4, part), jnp.float32)
    up_sums = jnp.zeros((shards, 4, block), jnp.float32)
    for grads, pre, which in (
        (qkv_grad_mine, pre_mine, seat),
        (qkv_grad_near, pre_near, near_seat),
    ):
        sums = jnp.sum(wide(grads), axis=1).reshape(3, part)[::2]
        qv_sums = lax.dynamic_update_index_in_dim(qv_sums, sums, which, 1)
        sums = jnp.sum(wide(pre), axis=0).reshape(shards, block)
        up_sums = lax.dynamic_update_index_in_dim(up_sums, sums, which, 1)
    out_sums = jnp.sum(wide(grad_attn).reshape(inputs.shape)[:, :own], axis=(0, 1))
    down_sums = jnp.sum(wide(grad_mlp).reshape(inputs.shape)[:, :own], axis=(0, 1))
    bias_sums = jnp.concatenate(
        [
            vector.reshape(shards, -1)
            for vector in (qv_sums, out_sums, up_sums, down_sums)
        ],
        axis=1,
    )
    vector = jnp.concatenate([grad_mod.reshape(-1), bias_sums.reshape(-1)])
    vector = vector + here.to_side(vector)
    grad_mod = vector[: count * 6 * width]
    bias_sums = vector[count * 6 * width :]
    near = here.to_core(vector)
    bias_sums = (bias_sums + near[count * 6 * width :]).reshape(shards, -1)
    grad_mod = ordered(
        core == 0,
        grad_mod.reshape(1, count * 6 * width),
        near[: count * 6 * width].reshape(1, count * 6 * width),
        0,
    )
    mod_low = low(grad_mod).reshape(1, -1)
    sent = jnp.concatenate(
        [jnp.broadcast_to(wide(mod_low), (shards, mod_low.shape[1])), bias_sums], axis=1
    )
    got = here.exchange(sent)
    mod_all = low(got[:, : mod_low.shape[1]]).reshape(shards * micros, 6 * width)
    bias_sums = jnp.sum(got[:, mod_low.shape[1] :], axis=0)
    cuts = []
    for vector in (qv_bias, out_bias, up_bias):
        cuts.append((cuts[-1] if cuts else 0) + vector.shape[0] // shards)
    grad_qv_bias, grad_out_bias, grad_up_bias, grad_down_bias = jnp.split(bias_sums, cuts)
    grad_mod_weight = contract(cond_rows, mod_all, 0, 0)
    span = 6 * width // shards
    grad_mod_bias = jnp.sum(
        wide(lax.dynamic_slice_in_dim(mod_all, here.shard * span, span, 1)), axis=0
    )
    grad_low = contract(mod_all, mod_weight, 1, 1).reshape(shards, micros, rows)
    grad_low = here.exchange(grad_low).transpose(1, 0, 2).reshape(micros, width)
    _, silu_pull = jax.vjp(jax.nn.silu, wide(condition))
    grad_condition = silu_pull(grad_low)[0]

    grad_qkv = wide(here.share(grad_qkv)).reshape(4, rows, 3, part)
    grad_qkv = grad_qkv.transpose(1, 2, 0, 3).reshape(rows, 3 * width)
    grad_out = wide(here.share(grad_out)).transpose(1, 0, 2).reshape(rows, width)
    grad_up = wide(here.share(grad_up)).reshape(4, rows, shards, block)
    grad_up = grad_up.transpose(1, 2, 0, 3).reshape(rows, hidden)
    grad_down = wide(here.share(grad_down)).reshape(4 * block, width)

    return (
        mixed,
        grad_latents,
        grad_condition,
        grad_mod_weight,
        grad_mod_bias,
        grad_qkv,
        grad_qv_bias,
        grad_out,
        grad_out_bias,
        grad_up,
        grad_up_bias,
        grad_down,
        grad_down_bias,
    )


def solution(mesh):
    tokens = P("fsdp", "seq", None)
    matrix = P("fsdp", None)
    vector = P("fsdp")
    parameters = (matrix, vector) * 5
    in_specs = (tokens, matrix) + parameters + (tokens,)
    out_specs = (tokens, tokens, matrix) + parameters
    return jax.shard_map(
        per_device, mesh=mesh, in_specs=in_specs, out_specs=out_specs, check_vma=False
    )
```

time: 2010 us -> 612 us (0.30)
  blocking collectives: 727 us -> 0 us
  waiting for transfers between devices: 707 us -> 172 us
  matrix products: 228 us -> 117 us
  starting transfers between devices: 147 us -> 72.7 us
  local copies, waits for them, and re-layouts: 117 us -> 169 us
    unnamed x5 -> x0, blocking collectives: 688 us -> none
    all_gather x7 -> x0, waiting for transfers between devices: 588 us -> none  [the longest x1 174 us: per_device(): lax.all_gather(mod_weight, 'fsdp', axis=0, tiled=True)]
    ppermute x0 -> x72, waiting for transfers between devices: none -> 171 us  [the longest x24 70.6 us: to_line(): lax.ppermute(values, 'fsdp', [(i, (i + 2) % self.shards) for i in range(s...]
    dot_general x30, matrix products: 181 us -> 91.2 us  [the longest x20 77.3 us: contract(): lax.dot_general(left_side, right_side, (((left_dim,), (right_dim,)), ((),...]
    unnamed x20 -> x0, starting transfers between devices: 87.6 us -> none
    reduce_scatter x2 -> x0, waiting for transfers between devices: 67.2 us -> none  [the longest x1 67.2 us: per_device(): lax.psum_scatter(term_weight.astype(jnp.bfloat16), 'fsdp', scatter_dimens...]
    unnamed x363 -> x190, local copies, waits for them, and re-layouts: 78.1 us -> 17.8 us
    reshape x4 -> x30, local copies, waits for them, and re-layouts: 3.08 us -> 58.5 us  [the longest x3 20.6 us: per_device(): grad_up = grad_up.transpose(1, 2, 0, 3).reshape(rows, hidden)]
  transfers between devices with their start and end apart: 45 -> 76, of which waited for: 18 -> 32; matrix products, arithmetic and copies ran while one was open for 42% -> 54% of each run, Pallas kernels for 0% -> 0%
where the time goes in v1:
time: 612 us; the launch traced here: 600 us
  waiting for transfers between devices  172 us (28%)
  local copies, waits for them, and re-layouts  169 us (28%)
  matrix products  117 us (19%)
  starting transfers between devices  72.7 us (12%)
  other arithmetic  65.7 us (11%)
    dot_general x20, matrix products, contract(): lax.dot_general(left_side, right_side, (((left_dim,), (right_dim,)), ((),...  77.3 us
    ppermute x24, waiting for transfers between devices, to_line(): lax.ppermute(values, 'fsdp', [(i, (i + 2) % self.shards) for i in range(s...  70.6 us
    ppermute x20, waiting for transfers between devices, to_pair(): lax.ppermute(values, 'fsdp', [(i, i ^ 1) for i in range(self.shards)])  70.5 us
    ppermute x11, waiting for transfers between devices, to_side(): return lax.ppermute(values, 'seq', [(i, i ^ 2) for i in range(self.seats)])  30 us
    ppermute x20, starting transfers between devices, to_pair(): lax.ppermute(values, 'fsdp', [(i, i ^ 1) for i in range(self.shards)])  24.9 us
    reshape x3, local copies, waits for them, and re-layouts, per_device(): grad_up = grad_up.transpose(1, 2, 0, 3).reshape(rows, hidden)  20.6 us
    all_to_all x4, starting transfers between devices, exchange(): lax.all_to_all(values, 'fsdp', split_axis=0, concat_axis=0, tiled=True)  19.8 us
    dynamic_update_slice x16, local copies, waits for them, and re-layouts, gather(): lax.dynamic_update_index_in_dim(total, near, start + 1 - self.pair, 0)  18.4 us
  transfers between devices with their start and end apart: 76, of which 32 were waited for; matrix products, arithmetic and copies ran while one was open for 54% of the time, Pallas kernels for 0%

profile of v1, /device:TPU:0, one launch (start us, length us, event | category | flops | bytes accessed | tf_op | source)
XLA Modules:
  0.0 599.7 jit_solution(6312258213408860464)
XLA Ops:
  26.1 5.9 reshape.1400
  89.4 5.1 collective-permute-done.16
  98.9 5.3 collective-permute-done.28
  153.4 4.6 fusion.139
  167.8 4.6 fusion.138
  183.0 7.9 %collective-permute-done.10 = bf16[576,512]{1,0:T(8,128)(2,1)} collective-permute-done((bf16[576,512]{1,0:T(8,128)(2,1)S(1)}, bf16[576,512]{1,0:T(8,128)(2,1)}, u32[]{:S(2)}, u32[]{:S(2)}) %collective-permute-start.10) | collective-permute-done | bytes 589856 | tf_op jit(solution)/shard_map/ppermute | solution.py:71
  193.5 7.1 %rev.6 = bf16[576,1,2,256]{3,2,0,1:T(2,128)(2,1)} reverse(bf16[576,1,2,256]{3,2,0,1:T(2,128)(2,1)} %reshape.1397), dimensions={2} | reverse | bytes 1179648 | tf_op jit(solution)/shard_map/rev | solution.py:224
  201.8 6.0 %fusion.132 = (f32[512]{0:T(512)S(1)}, f32[512,1152]{1,0:T(8,128)S(1)}, f32[512,1152]{1,0:T(8,128)}) fusion(f32[1152]{0:T(1024)S(1)} %get-tuple-element.28, bf16[256,1152]{1,0:T(8,128)(2,1)} %bitcast.2, bf16[128,1152]{1,0:T(8,128)(2,1)S(1)} %bitcast.405, bf16[128,1152]{1,0:T(8,128)(2,1)S(1)} %bitcast.375, f32[1152]{0:T(1024)S(1)} %copy-done.69, ...), kind=kOutput, calls=%fused_computation.323 | convolution fusion | flops 1370160640 | bytes 9743361 | tf_op jit(solution)/shard_map/dot_general | solution.py:17
  213.4 6.2 %convert_reduce_fusion.2 = (f32[1152]{0:T(1024)S(1)}, bf16[512,1152]{1,0:T(8,128)(2,1)}) fusion(f32[512,1152]{1,0:T(8,128)S(1)} %convolution_add_fusion.4, bf16[1152,1152]{1,0:T(8,128)(2,1)} %bitcast.60, f32[1152]{0:T(1024)S(1)} %get-tuple-element.23, bf16[256,1152]{1,0:T(8,128)(2,1)} %bitcast.64, bf16[128,1152]{1,0:T(8,128)(2,1)S(1)} %bitcast.409, ...), kind=kOutput, calls=%fused_computation.52 | convolution fusion | flops 1374878592 | bytes 7382016 | tf_op jit(solution)/shard_map/dot_general | solution.py:17
  224.0 4.8 fusion.124
  236.5 4.9 convert_reduce_fusion.1
  251.7 5.0 convolution_convert_fusion.1
  260.4 4.6 convolution_convert_fusion
  267.9 8.2 %collective-permute-done.39 = bf16[512,1152]{1,0:T(8,128)(2,1)} collective-permute-done((bf16[512,1152]{1,0:T(8,128)(2,1)S(1)}, bf16[512,1152]{1,0:T(8,128)(2,1)}, u32[]{:S(2)}, u32[]{:S(2)}) %collective-permute-start.39) | collective-permute-done | bytes 1179680 | tf_op jit(solution)/shard_map/ppermute | solution.py:71
  280.7 5.2 multiply_bitcast_fusion.1
  312.3 5.2 fusion.19
  339.8 6.2 %all-to-all-start.2 = ((f32[8,1,14976]{2,1,0:T(1,128)}), f32[8,1,14976]{2,1,0:T(1,128)}, u32[]{:S(2)}, u32[]{:S(2)}) async-start(f32[8,1,14976]{2,1,0:T(1,128)} %all_to_all.23), calls=%async_computation.2 | async-start | bytes 958464 | tf_op jit(solution)/shard_map/all_to_all | solution.py:125
  390.7 5.6 collective-permute-done.55
  418.3 4.8 add_convert_fusion.2
  430.2 10.8 %collective-permute-done.59 = bf16[4,144,1152]{2,1,0:T(8,128)(2,1)} collective-permute-done((bf16[4,144,1152]{2,1,0:T(8,128)(2,1)}, bf16[4,144,1152]{2,1,0:T(8,128)(2,1)}, u32[]{:S(2)}, u32[]{:S(2)}) %collective-permute-start.59) | collective-permute-done | bytes 1327136 | tf_op jit(solution)/shard_map/ppermute | solution.py:74
  443.1 26.3 %collective-permute-done.66 = bf16[4,144,1152]{2,1,0:T(8,128)(2,1)} collective-permute-done((bf16[4,144,1152]{2,1,0:T(8,128)(2,1)}, bf16[4,144,1152]{2,1,0:T(8,128)(2,1)}, u32[]{:S(2)}, u32[]{:S(2)}) %collective-permute-start.66) | collective-permute-done | bytes 1327136 | tf_op jit(solution)/shard_map/ppermute | solution.py:74
  471.2 20.1 %collective-permute-done.45 = bf16[4,144,864]{2,1,0:T(8,128)(2,1)S(1)} collective-permute-done((bf16[4,144,864]{2,1,0:T(8,128)(2,1)S(1)}, bf16[4,144,864]{2,1,0:T(8,128)(2,1)S(1)}, u32[]{:S(2)}, u32[]{:S(2)}) %collective-permute-start.45) | collective-permute-done | bytes 995360 | tf_op jit(solution)/shard_map/ppermute | solution.py:74
  492.9 9.5 %collective-permute-done.46 = bf16[144,864]{1,0:T(8,128)(2,1)S(1)} collective-permute-done((bf16[144,864]{1,0:T(8,128)(2,1)S(1)}, bf16[144,864]{1,0:T(8,128)(2,1)S(1)}, u32[]{:S(2)}, u32[]{:S(2)}) %collective-permute-start.46) | collective-permute-done | bytes 248864 | tf_op jit(solution)/shard_map/ppermute | solution.py:77
  502.6 7.0 %collective-permute-done.61 = bf16[144,1152]{1,0:T(8,128)(2,1)S(1)} collective-permute-done((bf16[144,1152]{1,0:T(8,128)(2,1)S(1)}, bf16[144,1152]{1,0:T(8,128)(2,1)S(1)}, u32[]{:S(2)}, u32[]{:S(2)}) %collective-permute-start.61) | collective-permute-done | bytes 331808 | tf_op jit(solution)/shard_map/ppermute | solution.py:77
  509.7 12.5 %collective-permute-done.47 = bf16[144,864]{1,0:T(8,128)(2,1)S(1)} collective-permute-done((bf16[144,864]{1,0:T(8,128)(2,1)S(1)}, bf16[144,864]{1,0:T(8,128)(2,1)S(1)}, u32[]{:S(2)}, u32[]{:S(2)}) %collective-permute-start.47) | collective-permute-done | bytes 248864 | tf_op jit(solution)/shard_map/ppermute | solution.py:77
  522.8 12.1 %collective-permute-done.48 = bf16[144,864]{1,0:T(8,128)(2,1)S(1)} collective-permute-done((bf16[144,864]{1,0:T(8,128)(2,1)S(1)}, bf16[144,864]{1,0:T(8,128)(2,1)S(1)}, u32[]{:S(2)}, u32[]{:S(2)}) %collective-permute-start.48) | collective-permute-done | bytes 248864 | tf_op jit(solution)/shard_map/ppermute | solution.py:77
  544.5 6.8 %collective-permute-done.63 = bf16[144,1152]{1,0:T(8,128)(2,1)S(1)} collective-permute-done((bf16[144,1152]{1,0:T(8,128)(2,1)S(1)}, bf16[144,1152]{1,0:T(8,128)(2,1)S(1)}, u32[]{:S(2)}, u32[]{:S(2)}) %collective-permute-start.63) | collective-permute-done | bytes 331808 | tf_op jit(solution)/shard_map/ppermute | solution.py:71
  558.3 5.2 reshape.1469
  563.5 5.2 copy.94
  575.4 5.8 reshape.1473
  581.2 7.6 %copy.102 = f32[144,8,4,144]{3,2,1,0:T(4,128)} copy(f32[144,8,4,144]{3,1,0,2:T(8,128)} %bitcast.369) | data formatting | bytes 5308416 | tf_op jit(solution)/shard_map/reshape | solution.py:395
  588.7 7.2 %reshape.1459 = f32[144,4608]{1,0:T(8,128)} reshape(f32[144,8,4,144]{3,2,1,0:T(4,128)} %copy.102) | data formatting | bytes 5308416 | tf_op jit(solution)/shard_map/reshape | solution.py:395
  (565 shorter events, 353.6 us)
Async XLA Ops:
  4.3 64.5 %collective-permute-start.26 = (bf16[144,1152]{1,0:T(8,128)(2,1)}, bf16[144,1152]{1,0:T(8,128)(2,1)}, u32[]{:S(2)}, u32[]{:S(2)}) collective-permute-start(bf16[144,1152]{1,0:T(8,128)(2,1)} %get-tuple-element.42), channel_id=1, source_target_pairs={{0,4},{4,0},{8,12},{12,8},{16,20},{20,16},{24,28},{28,24},{1,5},{5... | collective-permute-start | bytes 995336 | tf_op jit(solution)/shard_map/ppermute | solution.py:74
  7.3 64.1 %collective-permute-start.27 = (bf16[144,1152]{1,0:T(8,128)(2,1)}, bf16[144,1152]{1,0:T(8,128)(2,1)}, u32[]{:S(2)}, u32[]{:S(2)}) collective-permute-start(bf16[144,1152]{1,0:T(8,128)(2,1)} %get-tuple-element.42), channel_id=1, source_target_pairs={{0,8},{4,12},{8,16},{12,20},{16,24},{20,28},{24,0},{28,4},{1,9},{5... | collective-permute-start | bytes 995336 | tf_op jit(solution)/shard_map/ppermute | solution.py:77
  10.9 44.0 %collective-permute-start.11 = (bf16[72,1152]{1,0:T(8,128)(2,1)}, bf16[72,1152]{1,0:T(8,128)(2,1)}, u32[]{:S(2)}, u32[]{:S(2)}) collective-permute-start(bf16[72,1152]{1,0:T(8,128)(2,1)} %get-tuple-element.60), channel_id=1, source_target_pairs={{0,4},{4,0},{8,12},{12,8},{16,20},{20,16},{24,28},{28,24},{1,5},{5... | collective-permute-start | bytes 497672 | tf_op jit(solution)/shard_map/ppermute | solution.py:74
  11.4 47.1 %collective-permute-start.12 = (bf16[72,1152]{1,0:T(8,128)(2,1)}, bf16[72,1152]{1,0:T(8,128)(2,1)}, u32[]{:S(2)}, u32[]{:S(2)}) collective-permute-start(bf16[72,1152]{1,0:T(8,128)(2,1)} %get-tuple-element.60), channel_id=1, source_target_pairs={{0,8},{4,12},{8,16},{12,20},{16,24},{20,28},{24,0},{28,4},{1,9},{5... | collective-permute-start | bytes 497672 | tf_op jit(solution)/shard_map/ppermute | solution.py:77
  15.5 29.7 %all-to-all-start = ((bf16[8,2,2160]{2,1,0:T(2,128)(2,1)}), bf16[8,2,2160]{2,1,0:T(2,128)(2,1)S(1)}, u32[]{:S(2)}, u32[]{:S(2)}) async-start(bf16[8,2,2160]{2,1,0:T(2,128)(2,1)} %reshape.1491), calls=%async_computation | async-start | bytes 139264 | tf_op jit(solution)/shard_map/all_to_all | solution.py:125
  23.8 36.3 %collective-permute-start.2 = (bf16[144,864]{1,0:T(8,128)(2,1)}, bf16[144,864]{1,0:T(8,128)(2,1)}, u32[]{:S(2)}, u32[]{:S(2)}) collective-permute-start(bf16[144,864]{1,0:T(8,128)(2,1)} %reshape.1387), channel_id=1, source_target_pairs={{0,4},{4,0},{8,12},{12,8},{16,20},{20,16},{24,28},{28,24},{1,5},{5... | collective-permute-start | bytes 746504 | tf_op jit(solution)/shard_map/ppermute | solution.py:74
  47.1 51.6 %all-to-all-start.1 = ((f32[8,1,6912]{2,1,0:T(1,128)}), f32[8,1,6912]{2,1,0:T(1,128)S(1)}, u32[]{:S(2)}, u32[]{:S(2)}) async-start(f32[8,1,6912]{2,1,0:T(1,128)} %copy.86), calls=%async_computation.1 | async-start | bytes 442368 | tf_op jit(solution)/shard_map/all_to_all | solution.py:125
  71.4 24.4 %collective-permute-start.4 = (bf16[144,864]{1,0:T(8,128)(2,1)S(1)}, bf16[144,864]{1,0:T(8,128)(2,1)S(1)}, u32[]{:S(2)}, u32[]{:S(2)}) collective-permute-start(bf16[144,864]{1,0:T(8,128)(2,1)S(1)} %collective-permute-done.3), channel_id=1, source_target_pairs={{0,4},{4,0},{8,12},{12,8},{16,20},{20,16},{24,28},{28,24},{1,5},{5... | collective-permute-start | bytes 746504 | tf_op jit(solution)/shard_map/ppermute | solution.py:74
  75.3 21.3 %collective-permute-start.5 = (bf16[144,864]{1,0:T(8,128)(2,1)S(1)}, bf16[144,864]{1,0:T(8,128)(2,1)S(1)}, u32[]{:S(2)}, u32[]{:S(2)}) collective-permute-start(bf16[144,864]{1,0:T(8,128)(2,1)S(1)} %collective-permute-done.3), channel_id=1, source_target_pairs={{0,8},{4,12},{8,16},{12,20},{16,24},{20,28},{24,0},{28,4},{1,9},{5... | collective-permute-start | bytes 746504 | tf_op jit(solution)/shard_map/ppermute | solution.py:77
  78.2 50.0 %collective-permute-start.38 = (bf16[1,256,1152]{2,1,0:T(8,128)(2,1)}, bf16[1,256,1152]{2,1,0:T(8,128)(2,1)}, u32[]{:S(2)}, u32[]{:S(2)}) collective-permute-start(bf16[1,256,1152]{2,1,0:T(8,128)(2,1)} %pad_maximum_fusion.6), channel_id=1, source_target_pairs={{0,2},{1,3},{2,0},{3,1},{4,6},{5,7},{6,4},{7,5},{8,10},{9,11},{10,... | collective-permute-start | bytes 1769480 | tf_op jit(solution)/shard_map/ppermute | solution.py:71
  81.4 41.5 %collective-permute-start.1 = (bf16[1,256,1152]{2,1,0:T(8,128)(2,1)}, bf16[1,256,1152]{2,1,0:T(8,128)(2,1)}, u32[]{:S(2)}, u32[]{:S(2)}) collective-permute-start(bf16[1,256,1152]{2,1,0:T(8,128)(2,1)} %pad_maximum_fusion.5), channel_id=1, source_target_pairs={{0,2},{1,3},{2,0},{3,1},{4,6},{5,7},{6,4},{7,5},{8,10},{9,11},{10,... | collective-permute-start | bytes 1769480 | tf_op jit(solution)/shard_map/ppermute | solution.py:71
  116.4 62.4 %collective-permute-start.18 = (bf16[8,72,1152]{2,1,0:T(8,128)(2,1)}, bf16[8,72,1152]{2,1,0:T(8,128)(2,1)}, u32[]{:S(2)}, u32[]{:S(2)}) collective-permute-start(bf16[8,72,1152]{2,1,0:T(8,128)(2,1)} %bitcast_dynamic-update-slice_fusion.21), channel_id=1, source_target_pairs={{0,1},{1,0},{2,3},{3,2},{4,5},{5,4},{6,7},{7,6},{8,9},{9,8},{10,11... | collective-permute-start | bytes 3981320 | tf_op jit(solution)/shard_map/ppermute | solution.py:68
  134.2 27.2 %collective-permute-start.32 = (bf16[144,1152]{1,0:T(8,128)(2,1)}, bf16[144,1152]{1,0:T(8,128)(2,1)}, u32[]{:S(2)}, u32[]{:S(2)}) collective-permute-start(bf16[144,1152]{1,0:T(8,128)(2,1)} %collective-permute-done.31), channel_id=1, source_target_pairs={{0,4},{4,0},{8,12},{12,8},{16,20},{20,16},{24,28},{28,24},{1,5},{5... | collective-permute-start | bytes 995336 | tf_op jit(solution)/shard_map/ppermute | solution.py:74
  137.8 39.2 %collective-permute-start.25 = (bf16[144,1152]{1,0:T(8,128)(2,1)}, bf16[144,1152]{1,0:T(8,128)(2,1)}, u32[]{:S(2)}, u32[]{:S(2)}) collective-permute-start(bf16[144,1152]{1,0:T(8,128)(2,1)} %collective-permute-done.24), channel_id=1, source_target_pairs={{0,4},{4,0},{8,12},{12,8},{16,20},{20,16},{24,28},{28,24},{1,5},{5... | collective-permute-start | bytes 995336 | tf_op jit(solution)/shard_map/ppermute | solution.py:74
  163.2 60.8 %collective-permute-start.34 = (bf16[1152,1152]{1,0:T(8,128)(2,1)}, bf16[1152,1152]{1,0:T(8,128)(2,1)}, u32[]{:S(2)}, u32[]{:S(2)}) collective-permute-start(bf16[1152,1152]{1,0:T(8,128)(2,1)} %bitcast.60), channel_id=1, source_target_pairs={{0,1},{1,0},{2,3},{3,2},{4,5},{5,4},{6,7},{7,6},{8,9},{9,8},{10,11... | collective-permute-start | bytes 7962632 | tf_op jit(solution)/shard_map/ppermute | solution.py:68
  178.7 41.2 %collective-permute-start.33 = (bf16[1152,1152]{1,0:T(8,128)(2,1)}, bf16[1152,1152]{1,0:T(8,128)(2,1)}, u32[]{:S(2)}, u32[]{:S(2)}) collective-permute-start(bf16[1152,1152]{1,0:T(8,128)(2,1)} %bitcast.50), channel_id=1, source_target_pairs={{0,1},{1,0},{2,3},{3,2},{4,5},{5,4},{6,7},{7,6},{8,9},{9,8},{10,11... | collective-permute-start | bytes 7962632 | tf_op jit(solution)/shard_map/ppermute | solution.py:68
  235.0 21.8 %collective-permute-start.35 = (bf16[1,256,1152]{2,1,0:T(8,128)(2,1)}, bf16[1,256,1152]{2,1,0:T(8,128)(2,1)}, u32[]{:S(2)}, u32[]{:S(2)}) collective-permute-start(bf16[1,256,1152]{2,1,0:T(8,128)(2,1)} %slice.230), channel_id=1, source_target_pairs={{0,2},{1,3},{2,0},{3,1},{4,6},{5,7},{6,4},{7,5},{8,10},{9,11},{10,... | collective-permute-start | bytes 1769480 | tf_op jit(solution)/shard_map/ppermute | solution.py:71
  249.2 26.9 %collective-permute-start.39 = (bf16[512,1152]{1,0:T(8,128)(2,1)S(1)}, bf16[512,1152]{1,0:T(8,128)(2,1)}, u32[]{:S(2)}, u32[]{:S(2)}) collective-permute-start(bf16[512,1152]{1,0:T(8,128)(2,1)S(1)} %fusion.9), channel_id=1, source_target_pairs={{0,2},{1,3},{2,0},{3,1},{4,6},{5,7},{6,4},{7,5},{8,10},{9,11},{10,... | collective-permute-start | bytes 3538952 | tf_op jit(solution)/shard_map/ppermute | solution.py:71
  256.8 145.5 %collective-permute-start.58 = (bf16[1152,1152]{1,0:T(8,128)(2,1)}, bf16[1152,1152]{1,0:T(8,128)(2,1)}, u32[]{:S(2)}, u32[]{:S(2)}) collective-permute-start(bf16[1152,1152]{1,0:T(8,128)(2,1)} %convolution_convert_fusion.1), channel_id=1, source_target_pairs={{0,1},{1,0},{2,3},{3,2},{4,5},{5,4},{6,7},{7,6},{8,9},{9,8},{10,11... | collective-permute-start | bytes 7962632 | tf_op jit(solution)/shard_map/ppermute | solution.py:68
  265.0 145.7 %collective-permute-start.65 = (bf16[1152,1152]{1,0:T(8,128)(2,1)}, bf16[1152,1152]{1,0:T(8,128)(2,1)}, u32[]{:S(2)}, u32[]{:S(2)}) collective-permute-start(bf16[1152,1152]{1,0:T(8,128)(2,1)} %convolution_convert_fusion), channel_id=1, source_target_pairs={{0,1},{1,0},{2,3},{3,2},{4,5},{5,4},{6,7},{7,6},{8,9},{9,8},{10,11... | collective-permute-start | bytes 7962632 | tf_op jit(solution)/shard_map/ppermute | solution.py:68
  333.5 84.8 %collective-permute-start.44 = (bf16[1152,864]{0,1:T(8,128)(2,1)}, bf16[1152,864]{0,1:T(8,128)(2,1)}, u32[]{:S(2)}, u32[]{:S(2)}) collective-permute-start(bf16[1152,864]{0,1:T(8,128)(2,1)} %convolution_convert_fusion.2), channel_id=1, source_target_pairs={{0,1},{1,0},{2,3},{3,2},{4,5},{5,4},{6,7},{7,6},{8,9},{9,8},{10,11... | collective-permute-start | bytes 5971976 | tf_op jit(solution)/shard_map/ppermute | solution.py:68
  339.8 20.5 %all-to-all-start.2 = ((f32[8,1,14976]{2,1,0:T(1,128)}), f32[8,1,14976]{2,1,0:T(1,128)}, u32[]{:S(2)}, u32[]{:S(2)}) async-start(f32[8,1,14976]{2,1,0:T(1,128)} %all_to_all.23), calls=%async_computation.2 | async-start | bytes 958464 | tf_op jit(solution)/shard_map/all_to_all | solution.py:125
  351.6 46.3 %collective-permute-start.41 = (f32[1,128,1152]{2,1,0:T(8,128)}, f32[1,128,1152]{2,1,0:T(8,128)}, u32[]{:S(2)}, u32[]{:S(2)}) collective-permute-start(f32[1,128,1152]{2,1,0:T(8,128)} %get-tuple-element.47), channel_id=1, source_target_pairs={{0,1},{1,0},{2,3},{3,2},{4,5},{5,4},{6,7},{7,6},{8,9},{9,8},{10,11... | collective-permute-start | bytes 1769480 | tf_op jit(solution)/shard_map/ppermute | solution.py:68
  408.7 32.3 %collective-permute-start.59 = (bf16[4,144,1152]{2,1,0:T(8,128)(2,1)}, bf16[4,144,1152]{2,1,0:T(8,128)(2,1)}, u32[]{:S(2)}, u32[]{:S(2)}) collective-permute-start(bf16[4,144,1152]{2,1,0:T(8,128)(2,1)} %dynamic-slice_bitcast_fusion.1), channel_id=1, source_target_pairs={{0,4},{4,0},{8,12},{12,8},{16,20},{20,16},{24,28},{28,24},{1,5},{5... | collective-permute-start | bytes 3981320 | tf_op jit(solution)/shard_map/ppermute | solution.py:74
  416.0 53.4 %collective-permute-start.66 = (bf16[4,144,1152]{2,1,0:T(8,128)(2,1)}, bf16[4,144,1152]{2,1,0:T(8,128)(2,1)}, u32[]{:S(2)}, u32[]{:S(2)}) collective-permute-start(bf16[4,144,1152]{2,1,0:T(8,128)(2,1)} %dynamic-slice_bitcast_fusion), channel_id=1, source_target_pairs={{0,4},{4,0},{8,12},{12,8},{16,20},{20,16},{24,28},{28,24},{1,5},{5... | collective-permute-start | bytes 3981320 | tf_op jit(solution)/shard_map/ppermute | solution.py:74
  428.5 62.7 %collective-permute-start.45 = (bf16[4,144,864]{2,1,0:T(8,128)(2,1)S(1)}, bf16[4,144,864]{2,1,0:T(8,128)(2,1)S(1)}, u32[]{:S(2)}, u32[]{:S(2)}) collective-permute-start(bf16[4,144,864]{2,1,0:T(8,128)(2,1)S(1)} %dynamic-slice_bitcast_fusion.2), channel_id=1, source_target_pairs={{0,4},{4,0},{8,12},{12,8},{16,20},{20,16},{24,28},{28,24},{1,5},{5... | collective-permute-start | bytes 2985992 | tf_op jit(solution)/shard_map/ppermute | solution.py:74
  443.1 48.5 %collective-permute-start.60 = (bf16[144,1152]{1,0:T(8,128)(2,1)S(1)}, bf16[144,1152]{1,0:T(8,128)(2,1)S(1)}, u32[]{:S(2)}, u32[]{:S(2)}) collective-permute-start(bf16[144,1152]{1,0:T(8,128)(2,1)S(1)} %dynamic-slice_bitcast_fusion.5), channel_id=1, source_target_pairs={{0,8},{4,12},{8,16},{12,20},{16,24},{20,28},{24,0},{28,4},{1,9},{5... | collective-permute-start | bytes 995336 | tf_op jit(solution)/shard_map/ppermute | solution.py:77
  471.1 20.7 %collective-permute-start.67 = (bf16[144,1152]{1,0:T(8,128)(2,1)S(1)}, bf16[144,1152]{1,0:T(8,128)(2,1)S(1)}, u32[]{:S(2)}, u32[]{:S(2)}) collective-permute-start(bf16[144,1152]{1,0:T(8,128)(2,1)S(1)} %dynamic-slice_bitcast_fusion.4), channel_id=1, source_target_pairs={{0,8},{4,12},{8,16},{12,20},{16,24},{20,28},{24,0},{28,4},{1,9},{5... | collective-permute-start | bytes 995336 | tf_op jit(solution)/shard_map/ppermute | solution.py:77
  491.9 30.5 %collective-permute-start.68 = (bf16[144,1152]{1,0:T(8,128)(2,1)S(1)}, bf16[144,1152]{1,0:T(8,128)(2,1)S(1)}, u32[]{:S(2)}, u32[]{:S(2)}) collective-permute-start(bf16[144,1152]{1,0:T(8,128)(2,1)S(1)} %fusion.64), channel_id=1, source_target_pairs={{0,8},{4,12},{8,16},{12,20},{16,24},{20,28},{24,0},{28,4},{1,9},{5... | collective-permute-start | bytes 995336 | tf_op jit(solution)/shard_map/ppermute | solution.py:77
  509.7 25.9 %collective-permute-start.62 = (bf16[144,1152]{1,0:T(8,128)(2,1)S(1)}, bf16[144,1152]{1,0:T(8,128)(2,1)S(1)}, u32[]{:S(2)}, u32[]{:S(2)}) collective-permute-start(bf16[144,1152]{1,0:T(8,128)(2,1)S(1)} %fusion.68), channel_id=1, source_target_pairs={{0,8},{4,12},{8,16},{12,20},{16,24},{20,28},{24,0},{28,4},{1,9},{5... | collective-permute-start | bytes 995336 | tf_op jit(solution)/shard_map/ppermute | solution.py:77
  552.2 20.1 %collective-permute-start.64 = (bf16[2,144,1152]{2,1,0:T(8,128)(2,1)}, bf16[2,144,1152]{2,1,0:T(8,128)(2,1)}, u32[]{:S(2)}, u32[]{:S(2)}) collective-permute-start(bf16[2,144,1152]{2,1,0:T(8,128)(2,1)} %maximum_select_fusion.6), channel_id=1, source_target_pairs={{0,1},{1,0},{2,3},{3,2},{4,5},{5,4},{6,7},{7,6},{8,9},{9,8},{10,11... | collective-permute-start | bytes 1990664 | tf_op jit(solution)/shard_map/ppermute | solution.py:68
  556.3 39.7 %collective-permute-start.71 = (bf16[2,144,1152]{2,1,0:T(8,128)(2,1)}, bf16[2,144,1152]{2,1,0:T(8,128)(2,1)}, u32[]{:S(2)}, u32[]{:S(2)}) collective-permute-start(bf16[2,144,1152]{2,1,0:T(8,128)(2,1)} %maximum_select_fusion.8), channel_id=1, source_target_pairs={{0,1},{1,0},{2,3},{3,2},{4,5},{5,4},{6,7},{7,6},{8,9},{9,8},{10,11... | collective-permute-start | bytes 1990664 | tf_op jit(solution)/shard_map/ppermute | solution.py:68
  (133 other events, 1873.2 us)
